TPU v7x, 32 devices: a whole 2x2x4 slice. The times are simulated.
32 devices in a mesh: groups: 2 (over y), row: 8 (over z, x), col: 2 (over core).
Axes of the slice: x: 2, y: 2, z: 4, core: 2. Of those that a mesh axis runs over, the one named last changes fastest.
Arguments:
- embeddings: bfloat16 [2048, 512], P(('groups', 'col', 'row')), parts along dimension 0, may hold values from -15 to 15
- noise: float32 [2048], P(('groups', 'col', 'row')), parts along dimension 0, may hold values from 0.5 to 2
- targets: float32 [16, 2048], P(None, ('groups', 'col', 'row')), parts along dimension 1, may hold values from -6 to 6
Outputs:
- weights_out: float32 [16, 2048], P(None, ('groups', 'col', 'row')), parts along dimension 1
- residual: float32 [16, 2048], P(None, ('groups', 'col', 'row')), parts along dimension 1
There are 2 independent parts, one for each index of `groups`. A program takes and returns all parts, laid end to end along the dimension named above; each array names one. Nothing has to cross between parts.
All inputs are finite; a program needn't handle non-finite values.
Results may differ from a plain program's by a relative error of at most 0.00065.
Values may be sent and summed in bfloat16 or wider, within the bound.
A program may use at most 64 MiB of HBM per device.

v0:
```python
import jax
import jax.numpy as jnp
from jax import lax
from jax.sharding import PartitionSpec as P

LAYERS = 5
ITERS = 2


def sample_norms(block):
    values = block.astype(jnp.float32)
    return jnp.mean(values * values, axis=1) + 1e-05


def kernel_block(left, right, left_norms, right_norms):
    sigma = jnp.dot(left, right.T, preferred_element_type=jnp.float32) / left.shape[1]
    scale = jnp.sqrt(left_norms[:, None] * right_norms[None, :])
    kernel = sigma
    for layer in range(LAYERS - 1):
        rho = jnp.clip(sigma / scale, -1.0, 1.0)
        angle = jnp.arccos(rho)
        sine = jnp.sqrt(jnp.maximum(1.0 - rho * rho, 0.0))
        sigma = scale / jnp.pi * (sine + (jnp.pi - angle) * rho)
        kernel = sigma + kernel * (jnp.pi - angle) / jnp.pi
    return kernel / LAYERS


def squares(vector):
    return lax.psum(jnp.sum(vector * vector, axis=1, keepdims=True), ("row", "col"))


def per_device(embeddings, noise, targets):
    row_block = lax.all_gather(embeddings, "col", axis=0, tiled=True)
    row_norms = sample_norms(row_block)
    column_block = lax.all_gather(embeddings, "row", axis=0, tiled=True)
    gram = kernel_block(row_block, column_block, row_norms, sample_norms(column_block))
    weights_out = jnp.zeros_like(targets)
    residual = targets
    direction = targets
    norm_now = squares(residual)
    for step in range(ITERS):
        gathered = lax.all_gather(direction, "row", axis=1, tiled=True)
        partial_sum = lax.dot_general(
            gathered,
            gram,
            (((1,), (1,)), ((), ())),
            precision=lax.Precision.HIGHEST,
            preferred_element_type=jnp.float32,
        )
        product = lax.psum_scatter(partial_sum, "col", scatter_dimension=1, tiled=True)
        image = product + noise[None, :] * direction
        curve = lax.psum(jnp.sum(direction * image, axis=1, keepdims=True), ("row", "col"))
        alpha = norm_now / curve
        weights_out = weights_out + alpha * direction
        residual = residual - alpha * image
        norm_next = squares(residual)
        direction = residual + norm_next / norm_now * direction
        norm_now = norm_next
    return (weights_out, residual)


def solution(mesh):
    in_specs = (
        P(("groups", "col", "row"), None),
        P(("groups", "col", "row")),
        P(None, ("groups", "col", "row")),
    )
    out_specs = (P(None, ("groups", "col", "row")), P(None, ("groups", "col", "row")))
    return jax.shard_map(
        per_device, mesh=mesh, in_specs=in_specs, out_specs=out_specs, check_vma=False
    )
```

profile of v0, /device:TPU:0, one launch (start us, length us, event | category | flops | bytes accessed | tf_op | source)
XLA Modules:
  0.0 230.1 jit_solution(13168866712585091805)
XLA Ops:
  7.2 0.0 copy-start.1
  7.2 0.0 reduce-scatter.7.cloned.1.call-start
  7.2 33.2 %all_gather.13 = bf16[512,512]{1,0:T(8,128)(2,1)S(1)} all-gather(bf16[64,512]{1,0:T(8,128)(2,1)} %param.3), channel_id=1, replica_groups=mesh['groups'=2,'row'=8,'col'=2] {'row'}, dimensions={0}, use_global_device_ids=true | all-gather | bytes 589824 | tf_op jit(solution)/shard_map/all_gather | solution.py:35
  40.4 0.0 copy-done.1
  40.5 1.9 all_gather.12
  42.3 0.2 multiply_reduce_fusion
  42.5 0.0 copy-start
  42.5 0.1 multiply_reduce_fusion.1
  42.7 0.6 copy-done
  43.2 30.5 %all-gather = f32[8,64,16]{1,2,0:T(8,128)S(1)} all-gather(f32[1,64,16]{1,2,0:T(8,128)S(1)} %bitcast.34), channel_id=1, replica_groups=mesh['groups'=2,'row'=8,'col'=2] {'row'}, dimensions={0}, use_global_device_ids=true | all-gather | bytes 36864 | tf_op jit(solution)/shard_map/all_gather | solution.py:42
  73.7 0.1 reshape.14
  73.8 3.0 %add_multiply_fusion = f32[128,512]{1,0:T(8,128)S(1)} fusion(bf16[128,512]{1,0:T(8,128)(2,1)S(1)} %all_gather.12, bf16[512,512]{1,0:T(8,128)(2,1)S(1)} %all_gather.13, f32[512]{0:T(512)S(1)} %multiply_add_fusion.4, f32[128]{0:T(128)S(1)} %multiply_add_fusion.5), kind=kOutput, calls=%fused_computation.4 | convolution fusion | flops 71303168 | bytes 920064 | tf_op jit(solution)/shard_map/dot_general | solution.py:16
  76.8 0.3 convolution_bitcast_fusion.1
  77.1 0.8 copy.9
  77.9 0.0 reduce-scatter.7.cloned.1.call-update
  77.9 0.0 reduce-scatter.9.cloned.1.call-start
  78.0 8.6 %reduce-scatter.7.cloned.1.call-done = f32[64,16]{1,0:T(8,128)} async-done(((f32[128,16]{1,0:T(8,128)}), f32[64,16]{1,0:T(8,128)}) %reduce-scatter.7.cloned.1.call-update) | async-done | bytes 4112
  86.6 0.0 copy-start.2
  86.6 0.8 copy.10
  87.4 0.0 copy-done.2
  87.4 0.1 multiply_reduce_fusion.4
  87.6 33.9 %all-reduce = (f32[16,1]{0,1:T(1,128)S(1)}, f32[16,1]{0,1:T(1,128)S(1)}) all-reduce(f32[16,1]{0,1:T(1,128)S(1)} %bitcast.39, f32[16,1]{0,1:T(1,128)S(1)} %bitcast.38), channel_id=1, replica_groups=mesh['groups'=2,'row'=8,'col'=2] {'row','col'}, use_global_device_ids=true, to_apply=%region_1.0 | all-reduce | flops 32 | bytes 256 | tf_op jit(solution)/shard_map/psum | solution.py:29
  121.5 0.2 multiply_reduce_fusion.3
  121.7 29.5 %psum.30 = f32[16,1]{0,1:T(1,128)S(1)} all-reduce(f32[16,1]{0,1:T(1,128)S(1)} %bitcast.40), channel_id=1, replica_groups=mesh['groups'=2,'row'=8,'col'=2] {'row','col'}, use_global_device_ids=true, to_apply=%region_8.9 | all-reduce | flops 16 | bytes 128 | tf_op jit(solution)/shard_map/psum | solution.py:29
  151.1 0.1 fusion.4
  151.2 30.5 %all-gather.1 = f32[8,64,16]{1,2,0:T(8,128)S(1)} all-gather(f32[1,64,16]{1,2,0:T(8,128)S(1)} %fusion.4), channel_id=1, replica_groups=mesh['groups'=2,'row'=8,'col'=2] {'row'}, dimensions={0}, use_global_device_ids=true | all-gather | bytes 36864 | tf_op jit(solution)/shard_map/all_gather | solution.py:42
  181.7 0.1 reshape.16
  181.8 1.0 convolution_bitcast_fusion
  182.8 0.0 reduce-scatter.9.cloned.1.call-update
  182.8 4.8 %reduce-scatter.9.cloned.1.call-done = f32[64,16]{1,0:T(8,128)} async-done(((f32[128,16]{1,0:T(8,128)}), f32[64,16]{1,0:T(8,128)}) %reduce-scatter.9.cloned.1.call-update) | async-done | bytes 4112
  187.7 0.8 copy.12
  188.5 0.2 multiply_reduce_fusion.2
  188.7 33.9 %psum.31 = f32[16,1]{0,1:T(1,128)S(1)} all-reduce(f32[16,1]{0,1:T(1,128)S(1)} %bitcast.41), channel_id=1, replica_groups=mesh['groups'=2,'row'=8,'col'=2] {'row','col'}, use_global_device_ids=true, to_apply=%region_11.12 | all-reduce | flops 16 | bytes 128 | tf_op jit(solution)/shard_map/psum | solution.py:52
  222.6 0.7 multiply_subtract_fusion
  (7 shorter events, 0.1 us)
Async XLA Ops:
  7.2 33.3 %copy-start.1 = (bf16[64,512]{1,0:T(8,128)(2,1)S(1)}, bf16[64,512]{1,0:T(8,128)(2,1)}, u32[]{:S(2)}) copy-start(bf16[64,512]{1,0:T(8,128)(2,1)} %param.3) | copy-start | bytes 196612
  7.2 79.4 %reduce-scatter.7.cloned.1.call-start = ((), (), s32[]{:S(2)}) async-start(), calls=%async_computation.2 | async-start | bytes 98304
  42.5 0.7 copy-start
  77.9 109.7 %reduce-scatter.9.cloned.1.call-start = ((), (), s32[]{:S(2)}) async-start(), calls=%async_computation.3 | async-start | bytes 98304
  86.6 0.8 copy-start.2
Sparse Core Ops, SparseCore 0:
  78.0 8.5 reduce-scatter.6
  182.9 4.6 reduce-scatter.8
where the time goes:
time: 230 us
  blocking collectives  193 us (84%)
  between operations  14.1 us (6%)
  waiting for transfers between devices  13.5 us (6%)
  matrix products  4.25 us (2%)
  local copies, waits for them, and re-layouts  3.21 us (1%)
    psum x2, blocking collectives, squares(): lax.psum(jnp.sum(vector * vector, axis=1, keepdims=True), ('row', 'col'))  63.4 us
    all_gather x2, blocking collectives, per_device(): gathered = lax.all_gather(direction, 'row', axis=1, tiled=True)  61 us
    psum x1, blocking collectives, per_device(): lax.psum(jnp.sum(direction * image, axis=1, keepdims=True), ('row', 'col'))  33.9 us
    all_gather x1, blocking collectives, per_device(): column_block = lax.all_gather(embeddings, 'row', axis=0, tiled=True)  33.2 us
    unnamed x4, waiting for transfers between devices  13.5 us
  transfers between devices with their start and end apart: 2, of which 2 were waited for; matrix products, arithmetic and copies ran while one was open for 0% of the time, Pallas kernels for 0%

commit v1 on v0

v1 whole, which is shorter than its diff:
```python
import functools
import math

import jax
import jax.numpy as jnp
from jax import lax
from jax.experimental import pallas as pl
from jax.experimental.pallas import tpu as pltpu
from jax.sharding import PartitionSpec as P

LAYERS = 5
MESH = pl.DeviceIdType.MESH
ARCCOS = (
    1.5707963050,
    -0.2145988016,
    0.0889789874,
    -0.0501743046,
    0.0308918810,
    -0.0170881256,
    0.0066700901,
    -0.0012624911,
)


def root(x):
    return x * lax.rsqrt(jnp.maximum(x, 1e-30))


def arccos_over_pi(x, root_one_minus):
    total = jnp.full_like(x, ARCCOS[-1] / math.pi)
    for coefficient in ARCCOS[-2::-1]:
        total = total * x + coefficient / math.pi
    return total * root_one_minus


def layers(first):
    rho = jnp.clip(first, -1.0, 1.0)
    kernel = first
    for layer in range(LAYERS - 1):
        size = jnp.abs(rho) if layer == 0 else rho
        rest = 1.0 - size
        angle = arccos_over_pi(size, root(rest))
        share = 1.0 - angle
        if layer == 0:
            share = jnp.where(rho < 0.0, angle, share)
        sigma = root(rest * (1.0 + size)) * (1.0 / math.pi) + share * rho
        kernel = sigma + kernel * share
        rho = jnp.minimum(sigma, 1.0)
    return kernel


def body(
    rows, e_ref, noise_ref, t_ref, w_ref, res_ref,
    ecol, erow, tsib, tall, khi, klo, part, psib, fall, vbuf, cbuf,
    e_send, e_recv, es_send, es_recv, ts_send, ts_recv, t_send, t_recv,
    p_send, p_recv, f_send, f_recv, c_send, c_recv,
):
    f32, bf16 = jnp.float32, jnp.bfloat16
    g, r, c = lax.axis_index("groups"), lax.axis_index("row"), lax.axis_index("col")
    per, width = e_ref.shape
    count = t_ref.shape[0]
    other = 1 - c
    sibling = (g, r, other)
    half = rows // 2
    partner = r + 1 - 2 * lax.rem(r, 2)
    mine = pl.ds(pl.multiple_of(c * per, per), per)

    def copy(src, dst, send, recv, device):
        return pltpu.make_async_remote_copy(
            src_ref=src, dst_ref=dst, send_sem=send, recv_sem=recv, device_id=device, device_id_type=MESH
        )

    def row_peer(k):
        return lax.rem(r + k, rows)

    barrier = pltpu.get_barrier_semaphore()
    for k in range(rows):
        for d in range(2):
            if k or d:
                pl.semaphore_signal(
                    barrier, inc=1, device_id=(g, row_peer(k), lax.rem(c + d, 2)), device_id_type=MESH
                )
    pl.semaphore_wait(barrier, 2 * rows - 1)

    sends = []

    def start(*args):
        one = copy(*args)
        one.start()
        sends.append(one)
        return one

    e_sibling = start(e_ref, erow.at[mine], es_send, es_recv, sibling)
    t_sibling = start(t_ref, tsib, ts_send, ts_recv, sibling)
    start(e_ref, ecol.at[r], e_send.at[0], e_recv.at[r], (g, partner, c))
    for k in range(1, half):
        start(e_ref, ecol.at[r], e_send.at[k], e_recv.at[r], (g, row_peer(2 * k), c))

    ecol[r] = e_ref[...]
    erow[mine, :] = e_ref[...]
    first = c == 0
    lane = lax.broadcasted_iota(jnp.int32, (count, 2 * per), 1)
    row = lax.broadcasted_iota(jnp.int32, (count, 2 * per), 0)

    def pick(x):
        return jnp.where(first, x[:, :per], x[:, per:])

    t_sibling.wait_recv()
    t_mine, t_other = t_ref[...], tsib[...]
    tall[r] = jnp.where(
        first, jnp.concatenate([t_mine, t_other], axis=1), jnp.concatenate([t_other, t_mine], axis=1)
    )
    for k in range(1, rows):
        start(tall.at[r], tall.at[r], t_send.at[k], t_recv.at[r], (g, row_peer(k), c))
    noise = noise_ref[...]
    empty = jnp.zeros_like(noise)
    noise = jnp.where(
        first, jnp.concatenate([noise, empty], axis=1), jnp.concatenate([empty, noise], axis=1)
    )

    e_sibling.wait_recv()
    dims = (((1,), (1,)), ((), ()))
    block = erow[...]
    square = lax.dot_general(block, block, dims, preferred_element_type=f32)
    at = lax.broadcasted_iota(jnp.int32, square.shape, 0) == lax.broadcasted_iota(jnp.int32, square.shape, 1)
    row_norms = jnp.sum(jnp.where(at, square, 0.0), axis=0, keepdims=True) / width + 1e-05
    row_inverse = lax.rsqrt(row_norms)
    row_scale = row_norms * row_inverse / LAYERS
    row_inverse = row_inverse / width

    def gram(s):
        piece = ecol[s]
        sigma = lax.dot_general(piece, erow[...], dims, preferred_element_type=f32)
        wide = piece.astype(f32)
        norms = jnp.sum(wide * wide, axis=1, keepdims=True) / width + 1e-05
        inverse = lax.rsqrt(norms)
        kernel = layers(sigma * inverse * row_inverse)
        kernel = kernel * (norms * inverse) * row_scale
        high = kernel.astype(bf16)
        place = pl.ds(pl.multiple_of(s * per, per), per)
        khi[place, :] = high
        klo[place, :] = (kernel - high.astype(f32)).astype(bf16)

    def arrived(s):
        copy(e_ref, ecol.at[s], e_send.at[0], e_recv.at[s], (g, partner, c)).wait_recv()

    gram(r)
    arrived(partner)
    gram(partner)
    for k in range(1, half):
        s = row_peer(rows - 2 * k)
        arrived(s)
        start(ecol.at[s], ecol.at[s], e_send.at[half + k], e_recv.at[s], (g, partner, c))
        gram(s)
    for k in range(1, half):
        s = lax.rem(partner + rows - 2 * k, rows)
        arrived(s)
        gram(s)

    for k in range(1, rows):
        s = row_peer(k)
        copy(tall.at[r], tall.at[s], t_send.at[k], t_recv.at[s], (g, s, c)).wait_recv()

    def columns(vector):
        for k in range(half):
            a, b = vector[2 * k], vector[2 * k + 1]
            a = jnp.where(first, a, pltpu.roll(a, per, 1))
            b = jnp.where(first, pltpu.roll(b, per, 1), b)
            vbuf[:, 2 * per * k : 2 * per * (k + 1)] = jnp.where(lane < per, a, b)

    def apply(own):
        v = vbuf[...]
        high = v.astype(bf16)
        low = (v - high.astype(f32)).astype(bf16)
        both = jnp.concatenate([high, low], axis=0)
        a = jnp.dot(both, khi[...], preferred_element_type=f32)
        b = jnp.dot(high, klo[...], preferred_element_type=f32)
        return a[:count] + a[count:] + b + noise * own

    def total(x):
        return jnp.sum(jnp.sum(x, axis=0), axis=1, keepdims=True)

    targets = tall[...]
    columns(targets)
    own_targets = tall[r]
    mine_part = apply(own_targets)
    part[0] = mine_part
    p_one = start(part.at[0], psib.at[0], p_send.at[0], p_recv.at[0], sibling)
    p_one.wait_recv()
    fall[r] = mine_part + psib[0]
    for k in range(1, rows):
        start(fall.at[r], fall.at[r], f_send.at[k], f_recv.at[r], (g, row_peer(k), c))
    norm_zero = total(targets * targets)
    for k in range(1, rows):
        s = row_peer(k)
        copy(fall.at[r], fall.at[s], f_send.at[k], f_recv.at[s], (g, s, c)).wait_recv()
    image = fall[...]
    alpha = norm_zero / total(targets * image)
    residual = targets - alpha[None] * image
    norm_one = total(residual * residual)
    beta = norm_one / norm_zero

    columns(residual + beta[None] * targets)
    own_residual = own_targets - alpha * fall[r]
    own_direction = own_residual + beta * own_targets
    mine_part = apply(own_direction)
    part[1] = mine_part
    p_two = start(part.at[1], psib.at[1], p_send.at[1], p_recv.at[1], sibling)
    curve = jnp.sum(own_direction * mine_part, axis=1, keepdims=True)
    me = 2 * r + c
    cbuf[me] = jnp.sum(jnp.where(lane == row, curve, 0.0), axis=0, keepdims=True)
    for k in range(rows):
        for d in range(2):
            if k or d:
                start(
                    cbuf.at[me], cbuf.at[me], c_send.at[2 * k + d], c_recv.at[me],
                    (g, row_peer(k), lax.rem(c + d, 2)),
                )
    p_two.wait_recv()
    image = mine_part + psib[1]
    for k in range(rows):
        for d in range(2):
            if k or d:
                s = 2 * row_peer(k) + lax.rem(c + d, 2)
                copy(cbuf.at[me], cbuf.at[s], c_send.at[0], c_recv.at[s], sibling).wait_recv()
    curve = jnp.sum(cbuf[...], axis=0)
    curve = jnp.sum(jnp.where(lane == row, curve, 0.0), axis=1, keepdims=True)
    step = norm_one / curve
    w_ref[...] = pick(alpha * own_targets + step * own_direction)
    res_ref[...] = pick(own_residual - step * image)
    for one in sends:
        one.wait_send()


def per_device(rows, embeddings, noise, targets):
    per, width = embeddings.shape
    count = targets.shape[0]
    f32, bf16 = jnp.float32, jnp.bfloat16
    dma = pltpu.SemaphoreType.DMA
    vmem = pl.BlockSpec(memory_space=pltpu.VMEM)
    return pl.pallas_call(
        functools.partial(body, rows),
        out_shape=[jax.ShapeDtypeStruct((count, per), f32)] * 2,
        in_specs=[vmem] * 3,
        out_specs=[vmem] * 2,
        scratch_shapes=[
            pltpu.VMEM((rows, per, width), bf16),
            pltpu.VMEM((2 * per, width), bf16),
            pltpu.VMEM((count, per), f32),
            pltpu.VMEM((rows, count, 2 * per), f32),
            pltpu.VMEM((rows * per, 2 * per), bf16),
            pltpu.VMEM((rows * per, 2 * per), bf16),
            pltpu.VMEM((2, count, 2 * per), f32),
            pltpu.VMEM((2, count, 2 * per), f32),
            pltpu.VMEM((rows, count, 2 * per), f32),
            pltpu.VMEM((count, rows * per), f32),
            pltpu.VMEM((2 * rows, 1, 2 * per), f32),
            dma((rows,)), dma((rows,)), dma, dma, dma, dma, dma((rows,)), dma((rows,)),
            dma((2,)), dma((2,)), dma((rows,)), dma((rows,)), dma((2 * rows,)), dma((2 * rows,)),
        ],
        compiler_params=pltpu.CompilerParams(
            collective_id=0, has_side_effects=True, vmem_limit_bytes=40 * 2**20
        ),
    )(embeddings, noise.reshape(1, per), targets)


def solution(mesh):
    in_specs = (
        P(("groups", "col", "row"), None),
        P(("groups", "col", "row")),
        P(None, ("groups", "col", "row")),
    )
    out_specs = (P(None, ("groups", "col", "row")), P(None, ("groups", "col", "row")))
    return jax.shard_map(
        functools.partial(per_device, mesh.shape["row"]),
        mesh=mesh, in_specs=in_specs, out_specs=out_specs, check_vma=False,
    )
```

time: 230 us -> 32 us (0.14)
  blocking collectives: 193 us -> 0 us
  Pallas kernels: 0 us -> 27.7 us
  waiting for transfers between devices: 13.5 us -> 0 us
  between operations: 14.1 us -> 0.65 us
  matrix products: 4.25 us -> 0 us
    psum x3 -> x0, blocking collectives: 97.3 us -> none  [the longest x2 63.4 us: squares(): lax.psum(jnp.sum(vector * vector, axis=1, keepdims=True), ('row', 'col'))]
    all_gather x4 -> x0, blocking collectives: 96.1 us -> none  [the longest x2 61 us: per_device(): gathered = lax.all_gather(direction, 'row', axis=1, tiled=True)]
    pallas_call x0 -> x1, Pallas kernels: none -> 27.7 us  [per_device(): pl.pallas_call(functools.partial(body, rows), out_shape=[jax.ShapeDtypeSt...]
    unnamed x4 -> x0, waiting for transfers between devices: 13.5 us -> none
    dot_general x2 -> x0, matrix products: 3.28 us -> none  [the longest x1 3.01 us: kernel_block(): jnp.dot(left, right.T, preferred_element_type=jnp.float32) / left.shape[1]]
  transfers between devices with their start and end apart: 2 -> 0, of which waited for: 2 -> 0; matrix products, arithmetic and copies ran while one was open for 0% -> 0% of each run, Pallas kernels for 0% -> 0%
where the time goes in v1:
time: 32 us; the launch traced here: 31.7 us
  Pallas kernels  27.7 us (87%)
  local copies, waits for them, and re-layouts  3.38 us (11%)
  between operations  0.65 us (2%)
    pallas_call x1, Pallas kernels, per_device(): pl.pallas_call(functools.partial(body, rows), out_shape=[jax.ShapeDtypeSt...  27.7 us
    unnamed x8, local copies, waits for them, and re-layouts  3.38 us

profile of v1, /device:TPU:0, one launch (start us, length us, event | category | flops | bytes accessed | tf_op | source)
XLA Modules:
  0.0 31.7 jit_solution(13150247413571206004)
XLA Ops:
  0.6 0.0 copy-start.2
  0.6 0.6 %copy-done.2 = f32[64]{0:T(128)S(1)} copy-done((f32[64]{0:T(128)S(1)}, f32[64]{0:T(128)}, u32[]{:S(2)}) %copy-start.2) | copy-done | bytes 280
  1.3 0.0 copy-start
  1.3 0.8 %copy-done = bf16[64,512]{1,0:T(8,128)(2,1)S(1)} copy-done((bf16[64,512]{1,0:T(8,128)(2,1)S(1)}, bf16[64,512]{1,0:T(8,128)(2,1)}, u32[]{:S(2)}) %copy-start) | copy-done | bytes 65560
  2.1 0.0 copy-start.1
  2.1 0.7 %copy-done.1 = f32[16,64]{1,0:T(8,128)S(1)} copy-done((f32[16,64]{1,0:T(8,128)S(1)}, f32[16,64]{1,0:T(8,128)}, u32[]{:S(2)}) %copy-start.1) | copy-done | bytes 4120
  2.8 27.7 %shard_map.50 = (f32[16,64]{1,0:T(8,128)S(1)}, f32[16,64]{1,0:T(8,128)S(1)}) custom-call(bf16[64,512]{1,0:T(8,128)(2,1)S(1)} %copy-done, f32[1,64]{1,0:T(1,128)S(1)} %bitcast.1, f32[16,64]{1,0:T(8,128)S(1)} %copy-done.1), custom_call_target="tpu_custom_call" | custom-call | tf_op jit(solution)/shard_map/pallas_call | solution.py:241
  30.5 0.6 %copy.7 = f32[16,64]{1,0:T(8,128)} copy(f32[16,64]{1,0:T(8,128)S(1)} %get-tuple-element.4) | data formatting | bytes 8192
  31.1 0.6 %copy.8 = f32[16,64]{1,0:T(8,128)} copy(f32[16,64]{1,0:T(8,128)S(1)} %get-tuple-element.5) | data formatting | bytes 8192
Async XLA Ops:
  0.6 0.7 %copy-start.2 = (f32[64]{0:T(128)S(1)}, f32[64]{0:T(128)}, u32[]{:S(2)}) copy-start(f32[64]{0:T(128)} %param.4) | copy-start | bytes 772
  1.3 0.8 %copy-start = (bf16[64,512]{1,0:T(8,128)(2,1)S(1)}, bf16[64,512]{1,0:T(8,128)(2,1)}, u32[]{:S(2)}) copy-start(bf16[64,512]{1,0:T(8,128)(2,1)} %e_ref.1) | copy-start | bytes 196612
  2.1 0.7 %copy-start.1 = (f32[16,64]{1,0:T(8,128)S(1)}, f32[16,64]{1,0:T(8,128)}, u32[]{:S(2)}) copy-start(f32[16,64]{1,0:T(8,128)} %t_ref.1) | copy-start | bytes 12292

commit v2 on v1

--- a/solution.py
+++ b/solution.py
@@ -20,6 +20,14 @@
     0.0066700901,
     -0.0012624911,
 )
+
+
+def each(start, stop, step):
+    if stop - start <= 16:
+        for k in range(start, stop):
+            step(k)
+    else:
+        lax.fori_loop(start, stop, lambda k, _: (step(k), 0)[1], 0)
 
 
 def root(x):
@@ -50,8 +58,8 @@
 
 
 def body(
-    rows, e_ref, noise_ref, t_ref, w_ref, res_ref,
-    ecol, erow, tsib, tall, khi, klo, part, psib, fall, vbuf, cbuf,
+    rows, e_ref, noise_hbm, t_hbm, w_ref, res_ref,
+    noise_ref, t_ref, in_sem, ecol, erow, tsib, tall, khi, klo, part, psib, fall, vbuf, cbuf,
     e_send, e_recv, es_send, es_recv, ts_send, ts_recv, t_send, t_recv,
     p_send, p_recv, f_send, f_recv, c_send, c_recv,
 ):
@@ -63,7 +71,6 @@
     sibling = (g, r, other)
     half = rows // 2
     partner = r + 1 - 2 * lax.rem(r, 2)
-    mine = pl.ds(pl.multiple_of(c * per, per), per)
 
     def copy(src, dst, send, recv, device):
         return pltpu.make_async_remote_copy(
@@ -73,31 +80,50 @@
     def row_peer(k):
         return lax.rem(r + k, rows)
 
+    mine = pl.ds(pl.multiple_of(c * per, per), per)
+    loads = [
+        pltpu.make_async_copy(t_hbm, t_ref, in_sem.at[0]),
+        pltpu.make_async_copy(noise_hbm, noise_ref, in_sem.at[1]),
+        pltpu.make_async_copy(e_ref, ecol.at[r], in_sem.at[2]),
+        pltpu.make_async_copy(e_ref, erow.at[mine], in_sem.at[3]),
+    ]
+    for load in loads:
+        load.start()
+
     barrier = pltpu.get_barrier_semaphore()
-    for k in range(rows):
-        for d in range(2):
-            if k or d:
-                pl.semaphore_signal(
-                    barrier, inc=1, device_id=(g, row_peer(k), lax.rem(c + d, 2)), device_id_type=MESH
-                )
+
+    def everyone(step):
+        def one(j):
+            step(row_peer(j // 2), lax.rem(c + j % 2, 2), j)
+
+        each(1, 2 * rows, one)
+
+    everyone(
+        lambda s, d, j: pl.semaphore_signal(barrier, inc=1, device_id=(g, s, d), device_id_type=MESH)
+    )
     pl.semaphore_wait(barrier, 2 * rows - 1)
 
-    sends = []
-
-    def start(*args):
-        one = copy(*args)
-        one.start()
-        sends.append(one)
-        return one
-
-    e_sibling = start(e_ref, erow.at[mine], es_send, es_recv, sibling)
-    t_sibling = start(t_ref, tsib, ts_send, ts_recv, sibling)
-    start(e_ref, ecol.at[r], e_send.at[0], e_recv.at[r], (g, partner, c))
-    for k in range(1, half):
-        start(e_ref, ecol.at[r], e_send.at[k], e_recv.at[r], (g, row_peer(2 * k), c))
-
-    ecol[r] = e_ref[...]
-    erow[mine, :] = e_ref[...]
+    def e_direct(k):
+        return copy(e_ref, ecol.at[r], e_send.at[k], e_recv.at[r], (g, row_peer(2 * k), c))
+
+    def e_relay(k):
+        s = row_peer(rows - 2 * k)
+        return copy(ecol.at[s], ecol.at[s], e_send.at[half + k], e_recv.at[s], (g, partner, c))
+
+    def t_send_to(k):
+        return copy(tall.at[r], tall.at[r], t_send.at[k], t_recv.at[r], (g, row_peer(k), c))
+
+    def f_send_to(k):
+        return copy(fall.at[r], fall.at[r], f_send.at[k], f_recv.at[r], (g, row_peer(k), c))
+
+    e_sibling = copy(e_ref, erow.at[mine], es_send, es_recv, sibling)
+    e_partner = copy(e_ref, ecol.at[r], e_send.at[0], e_recv.at[r], (g, partner, c))
+    t_sibling = copy(t_ref, tsib, ts_send, ts_recv, sibling)
+    e_sibling.start()
+    each(1, half, lambda k: e_direct(k).start())
+    e_partner.start()
+    loads[0].wait()
+    t_sibling.start()
     first = c == 0
     lane = lax.broadcasted_iota(jnp.int32, (count, 2 * per), 1)
     row = lax.broadcasted_iota(jnp.int32, (count, 2 * per), 0)
@@ -110,8 +136,9 @@
     tall[r] = jnp.where(
         first, jnp.concatenate([t_mine, t_other], axis=1), jnp.concatenate([t_other, t_mine], axis=1)
     )
-    for k in range(1, rows):
-        start(tall.at[r], tall.at[r], t_send.at[k], t_recv.at[r], (g, row_peer(k), c))
+    each(1, rows, lambda k: t_send_to(k).start())
+    for load in loads[1:]:
+        load.wait()
     noise = noise_ref[...]
     empty = jnp.zeros_like(noise)
     noise = jnp.where(
@@ -147,19 +174,26 @@
     gram(r)
     arrived(partner)
     gram(partner)
-    for k in range(1, half):
+
+    def same_side(k):
         s = row_peer(rows - 2 * k)
         arrived(s)
-        start(ecol.at[s], ecol.at[s], e_send.at[half + k], e_recv.at[s], (g, partner, c))
+        e_relay(k).start()
         gram(s)
-    for k in range(1, half):
+
+    def far_side(k):
         s = lax.rem(partner + rows - 2 * k, rows)
         arrived(s)
         gram(s)
 
-    for k in range(1, rows):
+    each(1, half, same_side)
+    each(1, half, far_side)
+
+    def t_arrived(k):
         s = row_peer(k)
         copy(tall.at[r], tall.at[s], t_send.at[k], t_recv.at[s], (g, s, c)).wait_recv()
+
+    each(1, rows, t_arrived)
 
     def columns(vector):
         for k in range(half):
@@ -185,15 +219,18 @@
     own_targets = tall[r]
     mine_part = apply(own_targets)
     part[0] = mine_part
-    p_one = start(part.at[0], psib.at[0], p_send.at[0], p_recv.at[0], sibling)
+    p_one = copy(part.at[0], psib.at[0], p_send.at[0], p_recv.at[0], sibling)
+    p_one.start()
     p_one.wait_recv()
     fall[r] = mine_part + psib[0]
-    for k in range(1, rows):
-        start(fall.at[r], fall.at[r], f_send.at[k], f_recv.at[r], (g, row_peer(k), c))
+    each(1, rows, lambda k: f_send_to(k).start())
     norm_zero = total(targets * targets)
-    for k in range(1, rows):
+
+    def f_arrived(k):
         s = row_peer(k)
         copy(fall.at[r], fall.at[s], f_send.at[k], f_recv.at[s], (g, s, c)).wait_recv()
+
+    each(1, rows, f_arrived)
     image = fall[...]
     alpha = norm_zero / total(targets * image)
     residual = targets - alpha[None] * image
@@ -205,31 +242,42 @@
     own_direction = own_residual + beta * own_targets
     mine_part = apply(own_direction)
     part[1] = mine_part
-    p_two = start(part.at[1], psib.at[1], p_send.at[1], p_recv.at[1], sibling)
+    p_two = copy(part.at[1], psib.at[1], p_send.at[1], p_recv.at[1], sibling)
+    p_two.start()
     curve = jnp.sum(own_direction * mine_part, axis=1, keepdims=True)
     me = 2 * r + c
     cbuf[me] = jnp.sum(jnp.where(lane == row, curve, 0.0), axis=0, keepdims=True)
-    for k in range(rows):
-        for d in range(2):
-            if k or d:
-                start(
-                    cbuf.at[me], cbuf.at[me], c_send.at[2 * k + d], c_recv.at[me],
-                    (g, row_peer(k), lax.rem(c + d, 2)),
-                )
+
+    def c_send_to(s, d, j):
+        return copy(cbuf.at[me], cbuf.at[me], c_send.at[j], c_recv.at[me], (g, s, d))
+
+    everyone(lambda s, d, j: c_send_to(s, d, j).start())
     p_two.wait_recv()
     image = mine_part + psib[1]
-    for k in range(rows):
-        for d in range(2):
-            if k or d:
-                s = 2 * row_peer(k) + lax.rem(c + d, 2)
-                copy(cbuf.at[me], cbuf.at[s], c_send.at[0], c_recv.at[s], sibling).wait_recv()
+    everyone(
+        lambda s, d, j: copy(
+            cbuf.at[me], cbuf.at[2 * s + d], c_send.at[j], c_recv.at[2 * s + d], (g, s, d)
+        ).wait_recv()
+    )
     curve = jnp.sum(cbuf[...], axis=0)
     curve = jnp.sum(jnp.where(lane == row, curve, 0.0), axis=1, keepdims=True)
     step = norm_one / curve
     w_ref[...] = pick(alpha * own_targets + step * own_direction)
     res_ref[...] = pick(own_residual - step * image)
-    for one in sends:
+    for one in (e_sibling, e_partner, t_sibling, p_one, p_two):
         one.wait_send()
+
+    def sent(k):
+        t_send_to(k).wait_send()
+        f_send_to(k).wait_send()
+
+    def e_sent(k):
+        e_direct(k).wait_send()
+        e_relay(k).wait_send()
+
+    each(1, half, e_sent)
+    each(1, rows, sent)
+    everyone(lambda s, d, j: c_send_to(s, d, j).wait_send())
 
 
 def per_device(rows, embeddings, noise, targets):
@@ -241,9 +289,12 @@
     return pl.pallas_call(
         functools.partial(body, rows),
         out_shape=[jax.ShapeDtypeStruct((count, per), f32)] * 2,
-        in_specs=[vmem] * 3,
+        in_specs=[pl.BlockSpec(memory_space=pltpu.HBM)] * 3,
         out_specs=[vmem] * 2,
         scratch_shapes=[
+            pltpu.VMEM((1, per), f32),
+            pltpu.VMEM((count, per), f32),
+            dma((4,)),
             pltpu.VMEM((rows, per, width), bf16),
             pltpu.VMEM((2 * per, width), bf16),
             pltpu.VMEM((count, per), f32),

time: 32 us -> 32.2 us (level)
  no operation moved by 1% of the time
where the time goes in v2:
time: 32.2 us; the launch traced here: 31.9 us
  Pallas kernels  27.9 us (87%)
  local copies, waits for them, and re-layouts  3.38 us (10%)
  between operations  0.65 us (2%)
    pallas_call x1, Pallas kernels, per_device(): pl.pallas_call(functools.partial(body, rows), out_shape=[jax.ShapeDtypeSt...  27.9 us
    unnamed x8, local copies, waits for them, and re-layouts  3.38 us

profile of v2, /device:TPU:0, one launch (start us, length us, event | category | flops | bytes accessed | tf_op | source)
XLA Modules:
  0.0 31.9 jit_solution(5710088215257932208)
XLA Ops:
  0.6 0.0 copy-start.2
  0.6 0.6 %copy-done.2 = f32[64]{0:T(128)S(1)} copy-done((f32[64]{0:T(128)S(1)}, f32[64]{0:T(128)}, u32[]{:S(2)}) %copy-start.2) | copy-done | bytes 280
  1.3 0.0 copy-start
  1.3 0.8 %copy-done = bf16[64,512]{1,0:T(8,128)(2,1)S(1)} copy-done((bf16[64,512]{1,0:T(8,128)(2,1)S(1)}, bf16[64,512]{1,0:T(8,128)(2,1)}, u32[]{:S(2)}) %copy-start) | copy-done | bytes 65560
  2.1 0.0 copy-start.1
  2.1 0.7 %copy-done.1 = f32[16,64]{1,0:T(8,128)S(1)} copy-done((f32[16,64]{1,0:T(8,128)S(1)}, f32[16,64]{1,0:T(8,128)}, u32[]{:S(2)}) %copy-start.1) | copy-done | bytes 4120
  2.8 27.9 %shard_map.50 = (f32[16,64]{1,0:T(8,128)S(1)}, f32[16,64]{1,0:T(8,128)S(1)}) custom-call(bf16[64,512]{1,0:T(8,128)(2,1)S(1)} %copy-done, f32[1,64]{1,0:T(1,128)S(1)} %bitcast.1, f32[16,64]{1,0:T(8,128)S(1)} %copy-done.1), custom_call_target="tpu_custom_call" | custom-call | tf_op jit(solution)/shard_map/pallas_call | solution.py:289
  30.7 0.6 %copy.7 = f32[16,64]{1,0:T(8,128)} copy(f32[16,64]{1,0:T(8,128)S(1)} %get-tuple-element.4) | data formatting | bytes 8192
  31.3 0.6 %copy.8 = f32[16,64]{1,0:T(8,128)} copy(f32[16,64]{1,0:T(8,128)S(1)} %get-tuple-element.5) | data formatting | bytes 8192
Async XLA Ops:
  0.6 0.7 %copy-start.2 = (f32[64]{0:T(128)S(1)}, f32[64]{0:T(128)}, u32[]{:S(2)}) copy-start(f32[64]{0:T(128)} %param.4) | copy-start | bytes 772
  1.3 0.8 %copy-start = (bf16[64,512]{1,0:T(8,128)(2,1)S(1)}, bf16[64,512]{1,0:T(8,128)(2,1)}, u32[]{:S(2)}) copy-start(bf16[64,512]{1,0:T(8,128)(2,1)} %e_ref.1) | copy-start | bytes 196612
  2.1 0.7 %copy-start.1 = (f32[16,64]{1,0:T(8,128)S(1)}, f32[16,64]{1,0:T(8,128)}, u32[]{:S(2)}) copy-start(f32[16,64]{1,0:T(8,128)} %t_hbm.1) | copy-start | bytes 12292

commit v3 on v2

v3 whole, which is shorter than its diff:
```python
import functools
import math

import jax
import jax.numpy as jnp
from jax import lax
from jax.experimental import pallas as pl
from jax.experimental.pallas import tpu as pltpu
from jax.sharding import PartitionSpec as P

LAYERS = 5
MESH = pl.DeviceIdType.MESH
ARCCOS = (
    1.5707963050,
    -0.2145988016,
    0.0889789874,
    -0.0501743046,
    0.0308918810,
    -0.0170881256,
    0.0066700901,
    -0.0012624911,
)


def each(start, stop, step):
    if stop - start <= 16:
        for k in range(start, stop):
            step(k)
    else:
        lax.fori_loop(start, stop, lambda k, _: (step(k), 0)[1], 0)


def root(x):
    return x * lax.rsqrt(jnp.maximum(x, 1e-30))


def arccos_over_pi(x, root_one_minus):
    total = jnp.full_like(x, ARCCOS[-1] / math.pi)
    for coefficient in ARCCOS[-2::-1]:
        total = total * x + coefficient / math.pi
    return total * root_one_minus


def layers(first):
    rho = jnp.clip(first, -1.0, 1.0)
    kernel = first
    for layer in range(LAYERS - 1):
        size = jnp.abs(rho) if layer == 0 else rho
        rest = 1.0 - size
        angle = arccos_over_pi(size, root(rest))
        share = 1.0 - angle
        if layer == 0:
            share = jnp.where(rho < 0.0, angle, share)
        sigma = root(rest * (1.0 + size)) * (1.0 / math.pi) + share * rho
        kernel = sigma + kernel * share
        rho = jnp.minimum(sigma, 1.0)
    return kernel


def body(
    rows, e_ref, noise_hbm, t_hbm, w_ref, res_ref,
    noise_ref, t_ref, in_sem, line, plane, tpart, tall, khi, klo, parts, fall, dall, vbuf, pick, cbuf,
    e_send, e_recv, b_send, b_recv, tp_send, tp_recv, t_send, t_recv,
    p_send, p_recv, f_send, f_recv, c_send, c_recv,
):
    f32, bf16 = jnp.float32, jnp.bfloat16
    g, r, c = lax.axis_index("groups"), lax.axis_index("row"), lax.axis_index("col")
    per, width = e_ref.shape
    count = t_ref.shape[0]
    depth = rows // 2
    z, x = r // 2, lax.rem(r, 2)
    q = 2 * x + c
    wide = 4 * per

    def copy(src, dst, send, recv, device):
        return pltpu.make_async_remote_copy(
            src_ref=src, dst_ref=dst, send_sem=send, recv_sem=recv, device_id=device, device_id_type=MESH
        )

    def at_plane(k):
        p = lax.rem(q + k, 4)
        return p, (g, 2 * z + p // 2, lax.rem(p, 2))

    def at_line(k):
        s = lax.rem(z + k, depth)
        return s, (g, 2 * s + x, c)

    def place(p):
        return pl.ds(pl.multiple_of(p * per, per), per)

    loads = [
        pltpu.make_async_copy(t_hbm, t_ref, in_sem.at[0]),
        pltpu.make_async_copy(noise_hbm, noise_ref, in_sem.at[1]),
        pltpu.make_async_copy(e_ref, line.at[z], in_sem.at[2]),
        pltpu.make_async_copy(e_ref, plane.at[place(q)], in_sem.at[3]),
    ]
    for load in loads:
        load.start()

    barrier = pltpu.get_barrier_semaphore()

    def greet(device):
        pl.semaphore_signal(barrier, inc=1, device_id=device, device_id_type=MESH)

    each(1, depth, lambda k: greet(at_line(k)[1]))
    each(1, 4, lambda k: greet(at_plane(k)[1]))
    pl.semaphore_wait(barrier, depth + 2)

    def e_line(k):
        return copy(e_ref, line.at[z], e_send.at[k], e_recv.at[z], at_line(k)[1])

    def e_plane(k):
        return copy(e_ref, plane.at[place(q)], b_send.at[k], b_recv.at[q], at_plane(k)[1])

    def t_plane(k):
        return copy(t_ref, tpart.at[q], tp_send.at[k], tp_recv.at[q], at_plane(k)[1])

    def t_line(k):
        return copy(tall.at[z], tall.at[z], t_send.at[k], t_recv.at[z], at_line(k)[1])

    def p_plane(i, k):
        return copy(
            parts.at[i, q], parts.at[i, q], p_send.at[i, k], p_recv.at[i, q], at_plane(k)[1]
        )

    def f_line(k):
        return copy(fall.at[z], fall.at[z], f_send.at[k], f_recv.at[z], at_line(k)[1])

    each(1, depth, lambda k: e_line(k).start())
    each(1, 4, lambda k: e_plane(k).start())
    loads[0].wait()
    each(1, 4, lambda k: t_plane(k).start())
    for load in loads[1:]:
        load.wait()
    tpart[q] = t_ref[...]

    first = c == 0
    lane = lax.broadcasted_iota(jnp.int32, (count, 2 * per), 1)
    row = lax.broadcasted_iota(jnp.int32, (count, 2 * per), 0)
    spot = lax.broadcasted_iota(jnp.int32, (1, wide), 1) // per
    noise = noise_ref[...]
    noise = jnp.where(spot == q, jnp.concatenate([noise] * 4, axis=1), 0.0)

    def from_plane(k, source, target, send, recv):
        p, device = at_plane(k)
        copy(source, target(p), send.at[k], recv.at[p], device).wait_recv()

    def from_line(k, target, send, recv):
        s, device = at_line(k)
        copy(target.at[s], target.at[s], send.at[k], recv.at[s], device).wait_recv()

    each(1, 4, lambda k: from_plane(k, t_ref, lambda p: tpart.at[p], tp_send, tp_recv))
    tall[z] = jnp.concatenate([tpart[p] for p in range(4)], axis=1)
    each(1, depth, lambda k: t_line(k).start())

    each(1, 4, lambda k: from_plane(k, e_ref, lambda p: plane.at[place(p)], b_send, b_recv))
    dims = (((1,), (1,)), ((), ()))
    block = plane[...]
    square = lax.dot_general(block, block, dims, preferred_element_type=f32)
    at = lax.broadcasted_iota(jnp.int32, square.shape, 0) == lax.broadcasted_iota(jnp.int32, square.shape, 1)
    row_norms = jnp.sum(jnp.where(at, square, 0.0), axis=0, keepdims=True) / width + 1e-05
    row_inverse = lax.rsqrt(row_norms)
    row_scale = row_norms * row_inverse / LAYERS
    row_inverse = row_inverse / width

    def gram(s):
        piece = line[s]
        sigma = lax.dot_general(piece, plane[...], dims, preferred_element_type=f32)
        values = piece.astype(f32)
        norms = jnp.sum(values * values, axis=1, keepdims=True) / width + 1e-05
        inverse = lax.rsqrt(norms)
        kernel = layers(sigma * inverse * row_inverse)
        kernel = kernel * (norms * inverse) * row_scale
        high = kernel.astype(bf16)
        khi[place(s), :] = high
        klo[place(s), :] = (kernel - high.astype(f32)).astype(bf16)

    gram(z)

    def arrived(k):
        from_line(k, line, e_send, e_recv)
        gram(at_line(k)[0])

    each(1, depth, arrived)
    each(1, depth, lambda k: from_line(k, tall, t_send, t_recv))

    def columns(vector):
        side = pl.ds(pl.multiple_of(x * 2 * per, 2 * per), 2 * per)
        for k in range(depth // 2):
            a, b = vector[2 * k, :, side], vector[2 * k + 1, :, side]
            a = jnp.where(first, a, pltpu.roll(a, per, 1))
            b = jnp.where(first, pltpu.roll(b, per, 1), b)
            vbuf[:, 2 * per * k : 2 * per * (k + 1)] = jnp.where(lane < per, a, b)

    def apply(own):
        v = vbuf[...]
        high = v.astype(bf16)
        low = (v - high.astype(f32)).astype(bf16)
        both = jnp.concatenate([high, low], axis=0)
        a = jnp.dot(both, khi[...], preferred_element_type=f32)
        b = jnp.dot(high, klo[...], preferred_element_type=f32)
        return a[:count] + a[count:] + b + noise * own

    def total(values):
        return jnp.sum(jnp.sum(values, axis=0), axis=1, keepdims=True)

    def summed(i):
        each(1, 4, lambda k: from_plane(k, parts.at[i, q], lambda p: parts.at[i, p], p_send.at[i], p_recv.at[i]))
        return (parts[i, 0] + parts[i, 1]) + (parts[i, 2] + parts[i, 3])

    columns(tall)
    own_targets = tall[z]
    parts[0, q] = apply(own_targets)
    each(1, 4, lambda k: p_plane(0, k).start())
    targets = tall[...]
    norm_zero = total(targets * targets)
    own_image = summed(0)
    fall[z] = own_image
    each(1, depth, lambda k: f_line(k).start())
    each(1, depth, lambda k: from_line(k, fall, f_send, f_recv))
    image = fall[...]
    alpha = norm_zero / total(targets * image)
    residual = targets - alpha[None] * image
    norm_one = total(residual * residual)
    beta = norm_one / norm_zero

    dall[...] = residual + beta[None] * targets
    columns(dall)
    own_residual = own_targets - alpha * own_image
    own_direction = own_residual + beta * own_targets
    mine = apply(own_direction)
    curve = jnp.sum(own_direction * mine, axis=1, keepdims=True)
    me = 2 * r + c
    cbuf[me] = jnp.sum(jnp.where(lane == row, curve, 0.0), axis=0, keepdims=True)

    def everyone(step):
        def one(j):
            step(lax.rem(r + j // 2, rows), lax.rem(c + j % 2, 2), j)

        each(1, 2 * rows, one)

    def c_send_to(s, d, j):
        return copy(cbuf.at[me], cbuf.at[me], c_send.at[j], c_recv.at[me], (g, s, d))

    everyone(lambda s, d, j: c_send_to(s, d, j).start())
    parts[1, q] = mine
    each(1, 4, lambda k: p_plane(1, k).start())
    own_image = summed(1)
    everyone(
        lambda s, d, j: copy(
            cbuf.at[me], cbuf.at[2 * s + d], c_send.at[j], c_recv.at[2 * s + d], (g, s, d)
        ).wait_recv()
    )
    curve = jnp.sum(cbuf[...], axis=0)
    curve = jnp.sum(jnp.where(lane == row, curve, 0.0), axis=1, keepdims=True)
    step = norm_one / curve

    def own(values):
        pick[...] = values
        part = pick[:, pl.ds(pl.multiple_of(x * 2 * per, 2 * per), 2 * per)]
        return jnp.where(first, part[:, :per], part[:, per:])

    w_ref[...] = own(alpha * own_targets + step * own_direction)
    res_ref[...] = own(own_residual - step * own_image)

    def plane_sent(k):
        for one in (e_plane(k), t_plane(k), p_plane(0, k), p_plane(1, k)):
            one.wait_send()

    def line_sent(k):
        for one in (e_line(k), t_line(k), f_line(k)):
            one.wait_send()

    each(1, 4, plane_sent)
    each(1, depth, line_sent)
    everyone(lambda s, d, j: c_send_to(s, d, j).wait_send())


def per_device(rows, embeddings, noise, targets):
    per, width = embeddings.shape
    count = targets.shape[0]
    depth, wide = rows // 2, 4 * per
    f32, bf16 = jnp.float32, jnp.bfloat16
    dma = pltpu.SemaphoreType.DMA
    vmem = pl.BlockSpec(memory_space=pltpu.VMEM)
    return pl.pallas_call(
        functools.partial(body, rows),
        out_shape=[jax.ShapeDtypeStruct((count, per), f32)] * 2,
        in_specs=[pl.BlockSpec(memory_space=pltpu.HBM)] * 3,
        out_specs=[vmem] * 2,
        scratch_shapes=[
            pltpu.VMEM((1, per), f32),
            pltpu.VMEM((count, per), f32),
            dma((4,)),
            pltpu.VMEM((depth, per, width), bf16),
            pltpu.VMEM((wide, width), bf16),
            pltpu.VMEM((4, count, per), f32),
            pltpu.VMEM((depth, count, wide), f32),
            pltpu.VMEM((depth * per, wide), bf16),
            pltpu.VMEM((depth * per, wide), bf16),
            pltpu.VMEM((2, 4, count, wide), f32),
            pltpu.VMEM((depth, count, wide), f32),
            pltpu.VMEM((depth, count, wide), f32),
            pltpu.VMEM((count, depth * per), f32),
            pltpu.VMEM((count, wide), f32),
            pltpu.VMEM((2 * rows, 1, 2 * per), f32),
            dma((depth,)), dma((depth,)), dma((4,)), dma((4,)), dma((4,)), dma((4,)),
            dma((depth,)), dma((depth,)), dma((2, 4)), dma((2, 4)),
            dma((depth,)), dma((depth,)), dma((2 * rows,)), dma((2 * rows,)),
        ],
        compiler_params=pltpu.CompilerParams(
            collective_id=0, has_side_effects=True, vmem_limit_bytes=60 * 2**20
        ),
    )(embeddings, noise.reshape(1, per), targets)


def solution(mesh):
    in_specs = (
        P(("groups", "col", "row"), None),
        P(("groups", "col", "row")),
        P(None, ("groups", "col", "row")),
    )
    out_specs = (P(None, ("groups", "col", "row")), P(None, ("groups", "col", "row")))
    return jax.shard_map(
        functools.partial(per_device, mesh.shape["row"]),
        mesh=mesh, in_specs=in_specs, out_specs=out_specs, check_vma=False,
    )
```

time: 32.2 us -> 29.9 us (0.929)
  local copies, waits for them, and re-layouts: 3.38 us -> 1.9 us
  Pallas kernels: 27.9 us -> 27.2 us
    unnamed x8 -> x4, local copies, waits for them, and re-layouts: 3.38 us -> 1.9 us
    pallas_call x1, Pallas kernels: 27.9 us -> 27.2 us  [per_device(): pl.pallas_call(functools.partial(body, rows), out_shape=[jax.ShapeDtypeSt...]
where the time goes in v3:
time: 29.9 us; the launch traced here: 29.7 us
  Pallas kernels  27.2 us (91%)
  local copies, waits for them, and re-layouts  1.9 us (6%)
  between operations  0.65 us (2%)
    pallas_call x1, Pallas kernels, per_device(): pl.pallas_call(functools.partial(body, rows), out_shape=[jax.ShapeDtypeSt...  27.2 us
    unnamed x4, local copies, waits for them, and re-layouts  1.9 us

profile of v3, /device:TPU:0, one launch (start us, length us, event | category | flops | bytes accessed | tf_op | source)
XLA Modules:
  0.0 29.7 jit_solution(1745042252471525778)
XLA Ops:
  0.6 27.2 %shard_map.50 = (f32[16,64]{1,0:T(8,128)}, f32[16,64]{1,0:T(8,128)}) custom-call(bf16[64,512]{1,0:T(8,128)(2,1)} %e_ref.1, f32[1,64]{1,0:T(1,128)} %bitcast.1, f32[16,64]{1,0:T(8,128)} %t_hbm.1), custom_call_target="tpu_custom_call" | custom-call | tf_op jit(solution)/shard_map/pallas_call | solution.py:286
  27.8 0.0 copy-start
  27.8 1.3 %copy.7 = f32[16,64]{1,0:T(8,128)} copy(f32[16,64]{1,0:T(8,128)} %get-tuple-element.4) | data formatting | bytes 8192
  29.1 0.0 copy-done
  29.1 0.6 %copy.8 = f32[16,64]{1,0:T(8,128)} copy(f32[16,64]{1,0:T(8,128)S(1)} %copy-done) | data formatting | bytes 8192
Async XLA Ops:
  27.8 1.3 %copy-start = (f32[16,64]{1,0:T(8,128)S(1)}, f32[16,64]{1,0:T(8,128)}, u32[]{:S(2)}) copy-start(f32[16,64]{1,0:T(8,128)} %get-tuple-element.5) | copy-start | bytes 12292

commit v4 on v3

v4 whole, which is shorter than its diff:
```python
import functools
import math

import jax
import jax.numpy as jnp
from jax import lax
from jax.experimental import pallas as pl
from jax.experimental.pallas import tpu as pltpu
from jax.sharding import PartitionSpec as P

LAYERS = 5
MESH = pl.DeviceIdType.MESH
ARCCOS = (
    1.5707963050,
    -0.2145988016,
    0.0889789874,
    -0.0501743046,
    0.0308918810,
    -0.0170881256,
    0.0066700901,
    -0.0012624911,
)


def each(start, stop, step):
    if stop - start <= 16:
        for k in range(start, stop):
            step(k)
    else:
        lax.fori_loop(start, stop, lambda k, _: (step(k), 0)[1], 0)


def peer(me, k, count):
    if count & (count - 1):
        return lax.rem(me + k, count)
    found, bit = 0, 1
    while bit < count:
        mine, turn = lax.rem(me // bit, 2), (k // bit) % 2
        found, bit = found + bit * (mine + turn - 2 * mine * turn), 2 * bit
    return found


def root(x):
    return x * lax.rsqrt(jnp.maximum(x, 1e-30))


def arccos_over_pi(x, root_one_minus):
    total = jnp.full_like(x, ARCCOS[-1] / math.pi)
    for coefficient in ARCCOS[-2::-1]:
        total = total * x + coefficient / math.pi
    return total * root_one_minus


def layers(first):
    rho = jnp.clip(first, -1.0, 1.0)
    kernel = first
    for layer in range(LAYERS - 1):
        size = jnp.abs(rho) if layer == 0 else rho
        rest = 1.0 - size
        angle = arccos_over_pi(size, root(rest))
        share = 1.0 - angle
        if layer == 0:
            share = jnp.where(rho < 0.0, angle, share)
        sigma = root(rest * (1.0 + size)) * (1.0 / math.pi) + share * rho
        kernel = sigma + kernel * share
        rho = jnp.minimum(sigma, 1.0)
    return kernel


def body(
    rows, e_ref, noise_hbm, t_hbm, out_ref,
    noise_ref, t_ref, in_sem, line, plane, tsib, tline, khi, klo, part, psib, fall, dall, rest, pown, vbuf, cbuf,
    e_send, e_recv, b_send, b_recv, s_send, s_recv, t_send, t_recv,
    p_send, p_recv, f_send, f_recv, c_send, c_recv,
):
    f32, bf16 = jnp.float32, jnp.bfloat16
    g, r, c = lax.axis_index("groups"), lax.axis_index("row"), lax.axis_index("col")
    per, width = e_ref.shape
    count = t_ref.shape[0]
    some = count // 2
    depth = rows // 2
    z, x = r // 2, lax.rem(r, 2)
    q = 2 * x + c
    pair, wide = 2 * per, 4 * per
    other = 1 - c
    sibling = (g, r, other)

    def copy(src, dst, send, recv, device):
        return pltpu.make_async_remote_copy(
            src_ref=src, dst_ref=dst, send_sem=send, recv_sem=recv, device_id=device, device_id_type=MESH
        )

    def at_plane(k):
        p = peer(q, k, 4)
        return p, (g, 2 * z + p // 2, lax.rem(p, 2))

    def at_line(k):
        s = peer(z, k, depth)
        return s, (g, 2 * s + x, c)

    def at_row(k):
        s = peer(r, k, rows)
        return s, (g, s, c)

    def place(p):
        return pl.ds(pl.multiple_of(p * per, per), per)

    def side(p):
        return pl.ds(pl.multiple_of(p * pair, pair), pair)

    def share(d):
        return pl.ds(pl.multiple_of(d * some, some), some)

    loads = [
        pltpu.make_async_copy(t_hbm, t_ref, in_sem.at[0]),
        pltpu.make_async_copy(noise_hbm, noise_ref, in_sem.at[1]),
        pltpu.make_async_copy(e_ref, line.at[z], in_sem.at[2]),
        pltpu.make_async_copy(e_ref, plane.at[place(q)], in_sem.at[3]),
        pltpu.make_async_copy(t_hbm, tline.at[z], in_sem.at[4]),
    ]
    for load in loads:
        load.start()

    barrier = pltpu.get_barrier_semaphore()

    def greet(device):
        pl.semaphore_signal(barrier, inc=1, device_id=device, device_id_type=MESH)

    each(1, depth, lambda k: greet(at_line(k)[1]))
    each(1, 4, lambda k: greet(at_plane(k)[1]))
    pl.semaphore_wait(barrier, depth + 2)

    def e_line(k):
        return copy(e_ref, line.at[z], e_send.at[k], e_recv.at[z], at_line(k)[1])

    def e_plane(k):
        return copy(e_ref, plane.at[place(q)], b_send.at[k], b_recv.at[q], at_plane(k)[1])

    def t_row(k):
        return copy(t_hbm, tline.at[z], t_send.at[k], t_recv.at[z], at_line(k)[1])

    def t_from(k):
        s, device = at_line(k)
        return copy(t_hbm, tline.at[s], t_send.at[k], t_recv.at[s], device)

    def f_row(k):
        return copy(fall.at[r], fall.at[r], f_send.at[k], f_recv.at[r], at_row(k)[1])

    def f_from(k):
        s = at_row(k)[0]
        return copy(fall.at[s], fall.at[s], f_send.at[k], f_recv.at[s], at_row(k)[1])

    def p_plane(k):
        p, device = at_plane(k)
        return copy(part.at[1, :, side(p // 2)], pown.at[q], p_send.at[k], p_recv.at[q], device)

    def p_from(k):
        p, device = at_plane(k)
        return copy(pown.at[p], pown.at[p], p_send.at[k], p_recv.at[p], device)

    def between(i, src, dst):
        return copy(src, dst, s_send.at[i], s_recv.at[i], sibling)

    t_first = between(0, t_ref.at[share(other)], tsib)
    p_first = between(1, part.at[0, share(other)], psib)
    d_first = between(2, dall.at[c], dall.at[c])
    d_rest = between(3, rest.at[c], rest.at[c])

    each(1, depth, lambda k: e_line(depth - k).start())
    each(1, depth, lambda k: t_row(depth - k).start())
    each(1, 4, lambda k: e_plane(4 - k).start())
    loads[0].wait()
    t_first.start()

    first = c == 0
    lane = lax.broadcasted_iota(jnp.int32, (count, pair), 1)
    row = lax.broadcasted_iota(jnp.int32, (count, pair), 0)
    spot = lax.broadcasted_iota(jnp.int32, (1, wide), 1) // per

    for load in loads[1:]:
        load.wait()
    noise = noise_ref[...]
    noise = jnp.where(spot == q, jnp.concatenate([noise] * 4, axis=1), 0.0)

    def b_arrived(k):
        p, device = at_plane(k)
        copy(e_ref, plane.at[place(p)], b_send.at[k], b_recv.at[p], device).wait_recv()

    each(1, 4, b_arrived)
    dims = (((1,), (1,)), ((), ()))
    block = plane[...]
    square = lax.dot_general(block, block, dims, preferred_element_type=f32)
    at = lax.broadcasted_iota(jnp.int32, square.shape, 0) == lax.broadcasted_iota(jnp.int32, square.shape, 1)
    row_norms = jnp.sum(jnp.where(at, square, 0.0), axis=0, keepdims=True) / width + 1e-05
    row_inverse = lax.rsqrt(row_norms)
    row_scale = row_norms * row_inverse / LAYERS
    row_inverse = row_inverse / width

    def gram(s):
        piece = line[s]
        sigma = lax.dot_general(piece, plane[...], dims, preferred_element_type=f32)
        values = piece.astype(f32)
        norms = jnp.sum(values * values, axis=1, keepdims=True) / width + 1e-05
        inverse = lax.rsqrt(norms)
        kernel = layers(sigma * inverse * row_inverse)
        kernel = kernel * (norms * inverse) * row_scale
        high = kernel.astype(bf16)
        khi[place(s), :] = high
        klo[place(s), :] = (kernel - high.astype(f32)).astype(bf16)

    gram(z)
    t_mine = t_ref[share(c), :]
    t_first.wait_recv()
    t_other = tsib[...]
    fall[r, :, wide:] = jnp.where(
        first, jnp.concatenate([t_mine, t_other], axis=1), jnp.concatenate([t_other, t_mine], axis=1)
    )
    each(1, depth, lambda k: t_from(k).wait_recv())
    vbuf[...] = jnp.concatenate([tline[k] for k in range(depth)], axis=1)

    def arrived(k):
        s, device = at_line(k)
        copy(e_ref, line.at[s], e_send.at[k], e_recv.at[s], device).wait_recv()
        gram(s)

    each(1, depth, arrived)

    def whole(ref, s, lanes):
        return jnp.concatenate([ref[0, s, :, lanes], ref[1, s, :, lanes]], axis=0)

    def columns(ref):
        for k in range(depth // 2):
            a, b = whole(ref, 2 * k, side(x)), whole(ref, 2 * k + 1, side(x))
            a = jnp.where(first, a, pltpu.roll(a, per, 1))
            b = jnp.where(first, pltpu.roll(b, per, 1), b)
            vbuf[:, pair * k : pair * (k + 1)] = jnp.where(lane < per, a, b)

    def apply(own):
        v = vbuf[...]
        high = v.astype(bf16)
        low = (v - high.astype(f32)).astype(bf16)
        both = jnp.concatenate([high, low], axis=0)
        a = jnp.dot(both, khi[...], preferred_element_type=f32)
        b = jnp.dot(high, klo[...], preferred_element_type=f32)
        return a[:count] + a[count:] + b + noise * own

    def total(values):
        return jnp.sum(jnp.sum(values, axis=0), axis=1, keepdims=True)

    own_targets = t_ref[...]
    part[0] = apply(jnp.concatenate([own_targets] * 4, axis=1))
    p_first.start()
    p_first.wait_recv()
    fall[r, :, :wide] = part[0, share(c), :] + psib[...]
    each(1, rows, lambda k: f_row(rows - k).start())
    each(1, rows, lambda k: f_from(k).wait_recv())
    held = fall[...].reshape(depth, 2, some, wide + pair)
    image = held[:, 0, :, :wide] + held[:, 1, :, :wide]
    targets = jnp.concatenate([held[:, 0, :, wide:], held[:, 1, :, wide:]], axis=2)
    norm_zero = total(targets * targets)
    alpha = norm_zero / total(targets * image)
    residual = targets - alpha[None] * image
    norm_one = total(residual * residual)
    beta = norm_one / norm_zero
    dall[c] = residual + beta[None] * targets
    d_first.start()
    even, odd = fall[2 * z], fall[2 * z + 1]
    image = even[:, :wide] + odd[:, :wide]
    rest[c, 0] = jnp.concatenate([even[:, wide:], odd[:, wide:]], axis=1) - alpha * image
    rest[c, 1] = jnp.broadcast_to(alpha, (some, wide))
    rest[c, 2] = jnp.broadcast_to(norm_one, (some, wide))
    d_rest.start()
    d_first.wait_recv()

    columns(dall)
    own_direction = whole(dall, z, slice(None))
    mine = apply(own_direction)
    curve = jnp.sum(own_direction * mine, axis=1, keepdims=True)
    me = 2 * r + c
    cbuf[me] = jnp.sum(jnp.where(lane == row, curve, 0.0), axis=0, keepdims=True)

    def everyone(step):
        def one(j):
            j = 2 * rows - j
            other_me = peer(me, j, 2 * rows)
            step(other_me // 2, lax.rem(other_me, 2), j)

        each(1, 2 * rows, one)

    def c_send_to(s, d, j):
        return copy(cbuf.at[me], cbuf.at[me], c_send.at[j], c_recv.at[me], (g, s, d))

    everyone(lambda s, d, j: c_send_to(s, d, j).start())
    part[1] = mine
    each(1, 4, lambda k: p_plane(k).start())
    pown[q] = part[1, :, side(x)]
    d_rest.wait_recv()

    def own(values):
        return jnp.where(first, values[:, :per], values[:, per:])

    def own_rest(i):
        return own(jnp.concatenate([rest[0, i, :, side(x)], rest[1, i, :, side(x)]], axis=0))

    own_residual, alpha, norm_one = own_rest(0), own_rest(1), own_rest(2)
    own_direction = own(whole(dall, z, side(x)))
    own_weights = alpha * own_targets
    each(1, 4, lambda k: p_from(k).wait_recv())
    own_image = own((pown[0] + pown[1]) + (pown[2] + pown[3]))
    everyone(
        lambda s, d, j: copy(
            cbuf.at[me], cbuf.at[2 * s + d], c_send.at[j], c_recv.at[2 * s + d], (g, s, d)
        ).wait_recv()
    )
    curve = jnp.sum(cbuf[...], axis=0)
    curve = jnp.sum(jnp.where(lane == row, curve, 0.0), axis=1, keepdims=True)
    step = norm_one / curve
    out_ref[0] = own_weights + step * own_direction
    out_ref[1] = own_residual - step * own_image

    for one in (t_first, p_first, d_first, d_rest):
        one.wait_send()

    def plane_sent(k):
        e_plane(k).wait_send()
        p_plane(k).wait_send()

    def line_sent(k):
        e_line(k).wait_send()
        t_row(k).wait_send()

    def row_sent(k):
        f_row(k).wait_send()

    each(1, 4, plane_sent)
    each(1, depth, line_sent)
    each(1, rows, row_sent)
    everyone(lambda s, d, j: c_send_to(s, d, j).wait_send())


def per_device(rows, embeddings, noise, targets):
    per, width = embeddings.shape
    count = targets.shape[0]
    some, depth, pair, wide = count // 2, rows // 2, 2 * per, 4 * per
    f32, bf16 = jnp.float32, jnp.bfloat16
    dma = pltpu.SemaphoreType.DMA
    vmem = pl.BlockSpec(memory_space=pltpu.VMEM)
    out = pl.pallas_call(
        functools.partial(body, rows),
        out_shape=jax.ShapeDtypeStruct((2, count, per), f32),
        in_specs=[pl.BlockSpec(memory_space=pltpu.HBM)] * 3,
        out_specs=vmem,
        scratch_shapes=[
            pltpu.VMEM((1, per), f32),
            pltpu.VMEM((count, per), f32),
            dma((5,)),
            pltpu.VMEM((depth, per, width), bf16),
            pltpu.VMEM((wide, width), bf16),
            pltpu.VMEM((some, per), f32),
            pltpu.VMEM((depth, count, per), f32),
            pltpu.VMEM((depth * per, wide), bf16),
            pltpu.VMEM((depth * per, wide), bf16),
            pltpu.VMEM((2, count, wide), f32),
            pltpu.VMEM((some, wide), f32),
            pltpu.VMEM((rows, some, wide + pair), f32),
            pltpu.VMEM((2, depth, some, wide), f32),
            pltpu.VMEM((2, 3, some, wide), f32),
            pltpu.VMEM((4, count, pair), f32),
            pltpu.VMEM((count, depth * per), f32),
            pltpu.VMEM((2 * rows, 1, pair), f32),
            dma((depth,)), dma((depth,)), dma((4,)), dma((4,)), dma((4,)), dma((4,)),
            dma((depth,)), dma((depth,)), dma((4,)), dma((4,)),
            dma((rows,)), dma((rows,)), dma((2 * rows,)), dma((2 * rows,)),
        ],
        compiler_params=pltpu.CompilerParams(
            collective_id=0, has_side_effects=True, vmem_limit_bytes=60 * 2**20
        ),
    )(embeddings, noise.reshape(1, per), targets)
    return out[0], out[1]


def solution(mesh):
    in_specs = (
        P(("groups", "col", "row"), None),
        P(("groups", "col", "row")),
        P(None, ("groups", "col", "row")),
    )
    out_specs = (P(None, ("groups", "col", "row")), P(None, ("groups", "col", "row")))
    return jax.shard_map(
        functools.partial(per_device, mesh.shape["row"]),
        mesh=mesh, in_specs=in_specs, out_specs=out_specs, check_vma=False,
    )
```

time: 29.9 us -> 28.5 us (0.953)
  Pallas kernels: 27.2 us -> 26.4 us
  local copies, waits for them, and re-layouts: 1.9 us -> 1.32 us
    unnamed x4 -> x0, local copies, waits for them, and re-layouts: 1.9 us -> none
    squeeze x0 -> x1, local copies, waits for them, and re-layouts: none -> 1.32 us  [per_device(): return (out[0], out[1])]
    pallas_call x1, Pallas kernels: 27.2 us -> 26.4 us  [per_device(): pl.pallas_call(functools.partial(body, rows), out_shape=jax.ShapeDtypeStr...]
where the time goes in v4:
time: 28.5 us; the launch traced here: 28.3 us
  Pallas kernels  26.4 us (93%)
  local copies, waits for them, and re-layouts  1.32 us (5%)
  between operations  0.64 us (2%)
    pallas_call x1, Pallas kernels, per_device(): pl.pallas_call(functools.partial(body, rows), out_shape=jax.ShapeDtypeStr...  26.4 us
    squeeze x1, local copies, waits for them, and re-layouts, per_device(): return (out[0], out[1])  1.32 us

profile of v4, /device:TPU:0, one launch (start us, length us, event | category | flops | bytes accessed | tf_op | source)
XLA Modules:
  0.0 28.3 jit_solution(657522164297664149)
XLA Ops:
  0.6 26.4 %shard_map.50 = f32[2,16,64]{2,1,0:T(8,128)} custom-call(bf16[64,512]{1,0:T(8,128)(2,1)} %e_ref.1, f32[1,64]{1,0:T(1,128)} %bitcast.5, f32[16,64]{1,0:T(8,128)} %t_hbm.1), custom_call_target="tpu_custom_call" | custom-call | tf_op jit(solution)/shard_map/pallas_call | solution.py:348
  27.0 1.3 %slice_bitcast_fusion = (f32[16,64]{1,0:T(8,128)}, f32[16,64]{1,0:T(8,128)}) fusion(f32[2,16,64]{2,1,0:T(8,128)} %shard_map.50), kind=kLoop, calls=%fused_computation | loop fusion | bytes 16384 | tf_op jit(solution)/shard_map/squeeze | solution.py:379

commit v5 on v4

--- a/solution.py
+++ b/solution.py
@@ -166,9 +166,9 @@
     d_first = between(2, dall.at[c], dall.at[c])
     d_rest = between(3, rest.at[c], rest.at[c])
 
-    each(1, depth, lambda k: e_line(depth - k).start())
     each(1, depth, lambda k: t_row(depth - k).start())
     each(1, 4, lambda k: e_plane(4 - k).start())
+    each(1, depth, lambda k: e_line(k).start())
     loads[0].wait()
     t_first.start()
 

time: 28.5 us -> 27.6 us (0.968)
  Pallas kernels: 26.4 us -> 25.4 us
    pallas_call x1, Pallas kernels: 26.4 us -> 25.4 us  [per_device(): pl.pallas_call(functools.partial(body, rows), out_shape=jax.ShapeDtypeStr...]
where the time goes in v5:
time: 27.6 us; the launch traced here: 27.4 us
  Pallas kernels  25.4 us (92%)
  local copies, waits for them, and re-layouts  1.32 us (5%)
  between operations  0.64 us (2%)
    pallas_call x1, Pallas kernels, per_device(): pl.pallas_call(functools.partial(body, rows), out_shape=jax.ShapeDtypeStr...  25.4 us
    squeeze x1, local copies, waits for them, and re-layouts, per_device(): return (out[0], out[1])  1.32 us

profile of v5, /device:TPU:0, one launch (start us, length us, event | category | flops | bytes accessed | tf_op | source)
XLA Modules:
  0.0 27.4 jit_solution(14160472543912067554)
XLA Ops:
  0.6 25.4 %shard_map.50 = f32[2,16,64]{2,1,0:T(8,128)} custom-call(bf16[64,512]{1,0:T(8,128)(2,1)} %e_ref.1, f32[1,64]{1,0:T(1,128)} %bitcast.5, f32[16,64]{1,0:T(8,128)} %t_hbm.1), custom_call_target="tpu_custom_call" | custom-call | tf_op jit(solution)/shard_map/pallas_call | solution.py:348
  26.1 1.3 %slice_bitcast_fusion = (f32[16,64]{1,0:T(8,128)}, f32[16,64]{1,0:T(8,128)}) fusion(f32[2,16,64]{2,1,0:T(8,128)} %shard_map.50), kind=kLoop, calls=%fused_computation | loop fusion | bytes 16384 | tf_op jit(solution)/shard_map/squeeze | solution.py:379

commit v6 on v5

--- a/solution.py
+++ b/solution.py
@@ -118,16 +118,15 @@
         pltpu.make_async_copy(e_ref, plane.at[place(q)], in_sem.at[3]),
         pltpu.make_async_copy(t_hbm, tline.at[z], in_sem.at[4]),
     ]
+    barrier = pltpu.get_barrier_semaphore()
+
+    def greet(device):
+        pl.semaphore_signal(barrier, inc=1, device_id=device, device_id_type=MESH)
+
+    each(1, depth, lambda k: greet(at_line(depth - k)[1]))
+    each(1, 4, lambda k: greet(at_plane(4 - k)[1]))
     for load in loads:
         load.start()
-
-    barrier = pltpu.get_barrier_semaphore()
-
-    def greet(device):
-        pl.semaphore_signal(barrier, inc=1, device_id=device, device_id_type=MESH)
-
-    each(1, depth, lambda k: greet(at_line(k)[1]))
-    each(1, 4, lambda k: greet(at_plane(k)[1]))
     pl.semaphore_wait(barrier, depth + 2)
 
     def e_line(k):

time: 27.6 us -> 27.5 us (level)
  no operation moved by 1% of the time
where the time goes in v6:
time: 27.5 us; the launch traced here: 27.3 us
  Pallas kernels  25.4 us (92%)
  local copies, waits for them, and re-layouts  1.32 us (5%)
  between operations  0.64 us (2%)
    pallas_call x1, Pallas kernels, per_device(): pl.pallas_call(functools.partial(body, rows), out_shape=jax.ShapeDtypeStr...  25.4 us
    squeeze x1, local copies, waits for them, and re-layouts, per_device(): return (out[0], out[1])  1.32 us

profile of v6, /device:TPU:0, one launch (start us, length us, event | category | flops | bytes accessed | tf_op | source)
XLA Modules:
  0.0 27.3 jit_solution(12818083076754797796)
XLA Ops:
  0.6 25.4 %shard_map.50 = f32[2,16,64]{2,1,0:T(8,128)} custom-call(bf16[64,512]{1,0:T(8,128)(2,1)} %e_ref.1, f32[1,64]{1,0:T(1,128)} %bitcast.5, f32[16,64]{1,0:T(8,128)} %t_hbm.1), custom_call_target="tpu_custom_call" | custom-call | tf_op jit(solution)/shard_map/pallas_call | solution.py:347
  26.0 1.3 %slice_bitcast_fusion = (f32[16,64]{1,0:T(8,128)}, f32[16,64]{1,0:T(8,128)}) fusion(f32[2,16,64]{2,1,0:T(8,128)} %shard_map.50), kind=kLoop, calls=%fused_computation | loop fusion | bytes 16384 | tf_op jit(solution)/shard_map/squeeze | solution.py:378
